TPU v7x, 32 devices: a whole 2x2x4 slice. The times are simulated.
32 devices in a mesh: runs: 2 (over y), grp: 4 (over x, core), mem: 4 (over z).
Axes of the slice: x: 2, y: 2, z: 4, core: 2. Of those that a mesh axis runs over, the one named last changes fastest.
Arguments:
- coords: float32 [256, 3, 512], P(('runs', 'grp', 'mem')), parts along dimension 0, may hold values from 0 to 128, as said below
- noise: float32 [256, 512], P(('runs', 'grp', 'mem')), parts along dimension 0, may hold values from 0.2 to 1
- right_side: float32 [256, 512], P(('runs', 'grp', 'mem')), parts along dimension 0, may hold values from -11 to 11
- tiles: int32 [256, 4, 2], P(('runs', 'grp', 'mem')), parts along dimension 0, may hold values from 0 to 127, as said below
- tile_count: int32 [256], P(('runs', 'grp', 'mem')), parts along dimension 0, may hold values from 1 to 4
Outputs:
- solution: float32 [256, 512], P(('runs', 'grp', 'mem')), parts along dimension 0
- residual: float32 [256, 512], P(('runs', 'grp', 'mem')), parts along dimension 0
There are 2 independent parts, one for each index of `runs`. A program takes and returns all parts, laid end to end along the dimension named above; each array names one. Nothing has to cross between parts.
Inputs may be any that keep to these rules, and one draw needn't show every extreme that they name: `tiles`: slot k < tile_count[r] of block row r holds (r, r + k); the remaining slots hold (r, r). Every block c >= r whose kernel tile with r is nonzero is listed. `coords`: the time coordinate of block b lies in [k, k + 1) for an integer time cell k of the block; every block lies wholly in one time cell, cells are nondecreasing along the blocks, and each cell holds 1 to 2 consecutive blocks.
All inputs are finite; a program needn't handle non-finite values.
Results may differ from a plain program's by a relative error of at most 0.0003.
Values sent between devices are 32-bit elements; how exact they have to be, the bound alone decides.
No kernel may reach another device: no remote copies, remote signals or barrier semaphores. Data moves between devices by JAX's collectives and lax.ppermute only.
A program may use at most 64 MiB of HBM per device.

v0:
```python
import jax
import jax.numpy as jnp
from jax import lax
from jax.sharding import PartitionSpec as P

ITERS = 2


AMPLITUDE = 0.2
PRECISE = lax.Precision.HIGHEST


def from_behind(value, axis, by):
    length = lax.axis_size(axis)
    pairs = [(i, i + by) for i in range(length) if 0 <= i + by < length]
    return lax.ppermute(value, axis, pairs)


def wendland(distance):
    remain = jnp.maximum(1.0 - distance, 0.0)
    return remain**4 * (4.0 * distance + 1.0)


def tile_kernel(left, right):
    across_x = left[0][:, None] - right[0][None, :]
    across_y = left[1][:, None] - right[1][None, :]
    across_t = left[2][:, None] - right[2][None, :]
    spatial = jnp.sqrt(across_x * across_x + across_y * across_y)
    return AMPLITUDE * wendland(spatial) * wendland(jnp.abs(across_t))


def near_coord_window(coords, reach):
    beyond = from_behind(coords[: reach - 1], ("grp", "mem"), -1)
    return jnp.concatenate([coords, beyond], axis=0)


def near_vector_window(vector, reach):
    beyond = from_behind(vector[: reach - 1], ("grp", "mem"), -1)
    return jnp.concatenate([vector, beyond], axis=0)


def near_return(partial_value, blocks, reach):
    spilled = from_behind(partial_value[blocks:], ("grp", "mem"), 1)
    return partial_value[:blocks].at[: reach - 1].add(spilled)


def local_apply(window, coord_window, tiles, tile_count, base):
    blocks = tiles.shape[0]

    def row_step(block, partial_value):
        position = base + block
        own_vector = window[position]
        own_coords = coord_window[position]

        def tile_step(slot, partial_value):
            block_row = tiles[block, slot, 0]
            block_col = tiles[block, slot, 1]
            target = block_col - block_row + position
            kernel_tile = tile_kernel(own_coords, coord_window[target])
            partial_value = partial_value.at[position].add(
                jnp.dot(kernel_tile, window[target], precision=PRECISE)
            )
            mirror = jnp.where(block_col != block_row, 1.0, 0.0) * jnp.dot(
                own_vector, kernel_tile, precision=PRECISE
            )
            return partial_value.at[target].add(mirror)

        return lax.fori_loop(0, tile_count[block], tile_step, partial_value)

    return lax.fori_loop(0, blocks, row_step, jnp.zeros_like(window))


def squares(residual):
    return lax.psum(jnp.sum(residual * residual), ("grp", "mem"))


def local(coords, noise, right_side, tiles, tile_count):
    reach = tiles.shape[1]
    blocks = tiles.shape[0]
    base = 0
    coord_window = near_coord_window(coords, reach)
    solution = jnp.zeros_like(right_side)
    residual = right_side
    direction = right_side
    norm_now = squares(residual)
    for step in range(ITERS):
        window = near_vector_window(direction, reach)
        partial_value = local_apply(window, coord_window, tiles, tile_count, base)
        summed = near_return(partial_value, blocks, reach)
        image = noise * direction + summed
        curvature = lax.psum(jnp.sum(direction * image), ("grp", "mem"))
        image, curvature = (image, curvature)
        alpha = norm_now / curvature
        solution = solution + alpha * direction
        residual = residual - alpha * image
        if step + 1 < ITERS:
            norm_next = squares(residual)
            direction = residual + norm_next / norm_now * direction
            norm_now = norm_next
    return (solution, residual)


def solution(mesh):
    in_specs = (
        P(("runs", "grp", "mem"), None, None),
        P(("runs", "grp", "mem"), None),
        P(("runs", "grp", "mem"), None),
        P(("runs", "grp", "mem"), None, None),
        P(("runs", "grp", "mem")),
    )
    out_specs = (P(("runs", "grp", "mem"), None), P(("runs", "grp", "mem"), None))
    return jax.shard_map(local, mesh=mesh, in_specs=in_specs, out_specs=out_specs, check_vma=False)
```

profile of v0, /device:TPU:0, one launch (start us, length us, event | category | flops | bytes accessed | tf_op | source)
XLA Modules:
  0.0 706.2 jit_solution(13347024904326287897)
XLA Ops:
  4.0 5.8 collective-permute-done.1
  10.6 201.4 %while.79 = (s32[]{:T(128)}, f32[11,512]{1,0:T(8,128)S(1)}, s32[8]{0:T(128)S(1)}, f32[11,3,512]{2,1,0:T(4,128)S(1)}, f32[11,512]{1,0:T(8,128)S(1)}, /*index=5*/s...) while((s32[]{:T(128)}, f32[11,512]{1,0:T(8,128)S(1)}, ...), condition=%wide.region_7.8_spmd, body=%wide.region_2.7_spmd.sunk | while | flops 18352672 | bytes 95052 | solution.py:70
  11.4 30.5 %while.82 = (s32[]{:T(128)}, f32[11,512]{1,0:T(8,128)S(1)}, s32[]{:T(128)}, s32[2]{0:T(128)S(1)}, pred[2]{0:T(512)(128)(4,1)S(1)}, /*index=5*/s32[]{:T(128)}, f3...) while((s32[]{:T(128)}, f32[11,512]{1,0:T(8,128)S(1)}, ...), condition=%wide.region_6.6_spmd, body=%wide.region_3.5_spmd.sunk | while | flops 18352664 | bytes 78241 | solution.py:68
  14.1 1.7 fusion.55
  17.9 2.7 fusion.54
  27.9 2.7 fusion.54
  37.8 2.7 fusion.54
  42.8 20.6 %while.82 = (s32[]{:T(128)}, f32[11,512]{1,0:T(8,128)S(1)}, s32[]{:T(128)}, s32[2]{0:T(128)S(1)}, pred[2]{0:T(512)(128)(4,1)S(1)}, /*index=5*/s32[]{:T(128)}, f3...) while((s32[]{:T(128)}, f32[11,512]{1,0:T(8,128)S(1)}, ...), condition=%wide.region_6.6_spmd, body=%wide.region_3.5_spmd.sunk | while | flops 18352664 | bytes 78241 | solution.py:68
  49.3 2.7 fusion.54
  59.3 2.7 fusion.54
  64.3 20.6 %while.82 = (s32[]{:T(128)}, f32[11,512]{1,0:T(8,128)S(1)}, s32[]{:T(128)}, s32[2]{0:T(128)S(1)}, pred[2]{0:T(512)(128)(4,1)S(1)}, /*index=5*/s32[]{:T(128)}, f3...) while((s32[]{:T(128)}, f32[11,512]{1,0:T(8,128)S(1)}, ...), condition=%wide.region_6.6_spmd, body=%wide.region_3.5_spmd.sunk | while | flops 18352664 | bytes 78241 | solution.py:68
  70.8 2.7 fusion.54
  80.7 2.7 fusion.54
  85.7 20.6 %while.82 = (s32[]{:T(128)}, f32[11,512]{1,0:T(8,128)S(1)}, s32[]{:T(128)}, s32[2]{0:T(128)S(1)}, pred[2]{0:T(512)(128)(4,1)S(1)}, /*index=5*/s32[]{:T(128)}, f3...) while((s32[]{:T(128)}, f32[11,512]{1,0:T(8,128)S(1)}, ...), condition=%wide.region_6.6_spmd, body=%wide.region_3.5_spmd.sunk | while | flops 18352664 | bytes 78241 | solution.py:68
  92.2 2.7 fusion.54
  102.2 2.7 fusion.54
  107.2 30.5 %while.82 = (s32[]{:T(128)}, f32[11,512]{1,0:T(8,128)S(1)}, s32[]{:T(128)}, s32[2]{0:T(128)S(1)}, pred[2]{0:T(512)(128)(4,1)S(1)}, /*index=5*/s32[]{:T(128)}, f3...) while((s32[]{:T(128)}, f32[11,512]{1,0:T(8,128)S(1)}, ...), condition=%wide.region_6.6_spmd, body=%wide.region_3.5_spmd.sunk | while | flops 18352664 | bytes 78241 | solution.py:68
  113.7 2.7 fusion.54
  123.6 2.7 fusion.54
  133.5 2.7 fusion.54
  138.6 30.5 %while.82 = (s32[]{:T(128)}, f32[11,512]{1,0:T(8,128)S(1)}, s32[]{:T(128)}, s32[2]{0:T(128)S(1)}, pred[2]{0:T(512)(128)(4,1)S(1)}, /*index=5*/s32[]{:T(128)}, f3...) while((s32[]{:T(128)}, f32[11,512]{1,0:T(8,128)S(1)}, ...), condition=%wide.region_6.6_spmd, body=%wide.region_3.5_spmd.sunk | while | flops 18352664 | bytes 78241 | solution.py:68
  145.0 2.7 fusion.54
  155.0 2.7 fusion.54
  164.9 2.7 fusion.54
  169.9 20.6 %while.82 = (s32[]{:T(128)}, f32[11,512]{1,0:T(8,128)S(1)}, s32[]{:T(128)}, s32[2]{0:T(128)S(1)}, pred[2]{0:T(512)(128)(4,1)S(1)}, /*index=5*/s32[]{:T(128)}, f3...) while((s32[]{:T(128)}, f32[11,512]{1,0:T(8,128)S(1)}, ...), condition=%wide.region_6.6_spmd, body=%wide.region_3.5_spmd.sunk | while | flops 18352664 | bytes 78241 | solution.py:68
  176.4 2.7 fusion.54
  186.4 2.7 fusion.54
  191.4 20.6 %while.82 = (s32[]{:T(128)}, f32[11,512]{1,0:T(8,128)S(1)}, s32[]{:T(128)}, s32[2]{0:T(128)S(1)}, pred[2]{0:T(512)(128)(4,1)S(1)}, /*index=5*/s32[]{:T(128)}, f3...) while((s32[]{:T(128)}, f32[11,512]{1,0:T(8,128)S(1)}, ...), condition=%wide.region_6.6_spmd, body=%wide.region_3.5_spmd.sunk | while | flops 18352664 | bytes 78241 | solution.py:68
  197.9 2.7 fusion.54
  207.8 2.7 fusion.54
  212.0 63.6 %collective-permute-start.2 = (f32[3,512]{1,0:T(4,128)S(1)}, f32[3,512]{1,0:T(4,128)S(1)}, u32[]{:S(2)}, u32[]{:S(2)}) collective-permute-start(f32[3,512]{1,0:T(4,128)S(1)} %slice.199), channel_id=1, source_target_pairs={{0,1},{1,2},{2,3},{3,4},{4,5},{5,6},{6,7},{7,8},{8,9},{9,10},{10,1... | collective-permute-start | bytes 18440 | tf_op jit(solution)/shard_map/ppermute | solution.py:16
  277.7 57.6 %all-reduce = (f32[]{:T(128)}, f32[]{:T(128)}) all-reduce(f32[]{:T(128)} %get-tuple-element.603, f32[]{:T(128)} %get-tuple-element.602), channel_id=1, replica_groups=mesh['runs'=2,'grp'=4,'mem'=4] {'grp','mem'}, use_global_device_ids=true, to_apply=%region_1.0 | all-reduce | flops 2 | bytes 16 | tf_op jit(solution)/shard_map/psum | solution.py:74
  337.2 30.5 %psum.30 = f32[]{:T(128)} all-reduce(f32[]{:T(128)} %get-tuple-element.674), channel_id=1, replica_groups=mesh['runs'=2,'grp'=4,'mem'=4] {'grp','mem'}, use_global_device_ids=true, to_apply=%region_11.12 | all-reduce | flops 1 | bytes 8 | tf_op jit(solution)/shard_map/psum | solution.py:74
  370.4 4.2 collective-permute-done.3
  374.7 201.4 %while.81 = (s32[]{:T(128)}, f32[11,512]{1,0:T(8,128)S(1)}, s32[8]{0:T(128)S(1)}, f32[11,3,512]{2,1,0:T(4,128)S(1)}, f32[11,512]{1,0:T(8,128)S(1)}, /*index=5*/s...) while((s32[]{:T(128)}, f32[11,512]{1,0:T(8,128)S(1)}, ...), condition=%wide.region_17.0_spmd, body=%wide.region_12.17_spmd.sunk | while | flops 18352672 | bytes 95036 | solution.py:70
  375.5 30.5 %while.83 = (s32[]{:T(128)}, f32[11,512]{1,0:T(8,128)S(1)}, s32[]{:T(128)}, s32[2]{0:T(128)S(1)}, pred[2]{0:T(512)(128)(4,1)S(1)}, /*index=5*/s32[]{:T(128)}, f3...) while((s32[]{:T(128)}, f32[11,512]{1,0:T(8,128)S(1)}, ...), condition=%wide.region_16.0_spmd, body=%wide.region_13.15_spmd.sunk | while | flops 18352664 | bytes 78241 | solution.py:68
  382.0 2.7 fusion.49
  392.0 2.7 fusion.49
  401.9 2.7 fusion.49
  406.9 20.6 %while.83 = (s32[]{:T(128)}, f32[11,512]{1,0:T(8,128)S(1)}, s32[]{:T(128)}, s32[2]{0:T(128)S(1)}, pred[2]{0:T(512)(128)(4,1)S(1)}, /*index=5*/s32[]{:T(128)}, f3...) while((s32[]{:T(128)}, f32[11,512]{1,0:T(8,128)S(1)}, ...), condition=%wide.region_16.0_spmd, body=%wide.region_13.15_spmd.sunk | while | flops 18352664 | bytes 78241 | solution.py:68
  413.4 2.7 fusion.49
  423.4 2.7 fusion.49
  428.4 20.6 %while.83 = (s32[]{:T(128)}, f32[11,512]{1,0:T(8,128)S(1)}, s32[]{:T(128)}, s32[2]{0:T(128)S(1)}, pred[2]{0:T(512)(128)(4,1)S(1)}, /*index=5*/s32[]{:T(128)}, f3...) while((s32[]{:T(128)}, f32[11,512]{1,0:T(8,128)S(1)}, ...), condition=%wide.region_16.0_spmd, body=%wide.region_13.15_spmd.sunk | while | flops 18352664 | bytes 78241 | solution.py:68
  434.9 2.7 fusion.49
  444.8 2.7 fusion.49
  449.8 20.6 %while.83 = (s32[]{:T(128)}, f32[11,512]{1,0:T(8,128)S(1)}, s32[]{:T(128)}, s32[2]{0:T(128)S(1)}, pred[2]{0:T(512)(128)(4,1)S(1)}, /*index=5*/s32[]{:T(128)}, f3...) while((s32[]{:T(128)}, f32[11,512]{1,0:T(8,128)S(1)}, ...), condition=%wide.region_16.0_spmd, body=%wide.region_13.15_spmd.sunk | while | flops 18352664 | bytes 78241 | solution.py:68
  456.3 2.7 fusion.49
  466.2 2.7 fusion.49
  471.3 30.5 %while.83 = (s32[]{:T(128)}, f32[11,512]{1,0:T(8,128)S(1)}, s32[]{:T(128)}, s32[2]{0:T(128)S(1)}, pred[2]{0:T(512)(128)(4,1)S(1)}, /*index=5*/s32[]{:T(128)}, f3...) while((s32[]{:T(128)}, f32[11,512]{1,0:T(8,128)S(1)}, ...), condition=%wide.region_16.0_spmd, body=%wide.region_13.15_spmd.sunk | while | flops 18352664 | bytes 78241 | solution.py:68
  477.7 2.7 fusion.49
  487.7 2.7 fusion.49
  497.6 2.7 fusion.49
  502.7 30.5 %while.83 = (s32[]{:T(128)}, f32[11,512]{1,0:T(8,128)S(1)}, s32[]{:T(128)}, s32[2]{0:T(128)S(1)}, pred[2]{0:T(512)(128)(4,1)S(1)}, /*index=5*/s32[]{:T(128)}, f3...) while((s32[]{:T(128)}, f32[11,512]{1,0:T(8,128)S(1)}, ...), condition=%wide.region_16.0_spmd, body=%wide.region_13.15_spmd.sunk | while | flops 18352664 | bytes 78241 | solution.py:68
  509.1 2.7 fusion.49
  519.1 2.7 fusion.49
  529.0 2.7 fusion.49
  534.0 20.6 %while.83 = (s32[]{:T(128)}, f32[11,512]{1,0:T(8,128)S(1)}, s32[]{:T(128)}, s32[2]{0:T(128)S(1)}, pred[2]{0:T(512)(128)(4,1)S(1)}, /*index=5*/s32[]{:T(128)}, f3...) while((s32[]{:T(128)}, f32[11,512]{1,0:T(8,128)S(1)}, ...), condition=%wide.region_16.0_spmd, body=%wide.region_13.15_spmd.sunk | while | flops 18352664 | bytes 78241 | solution.py:68
  540.5 2.7 fusion.49
  550.5 2.7 fusion.49
  555.5 20.6 %while.83 = (s32[]{:T(128)}, f32[11,512]{1,0:T(8,128)S(1)}, s32[]{:T(128)}, s32[2]{0:T(128)S(1)}, pred[2]{0:T(512)(128)(4,1)S(1)}, /*index=5*/s32[]{:T(128)}, f3...) while((s32[]{:T(128)}, f32[11,512]{1,0:T(8,128)S(1)}, ...), condition=%wide.region_16.0_spmd, body=%wide.region_13.15_spmd.sunk | while | flops 18352664 | bytes 78241 | solution.py:68
  562.0 2.7 fusion.49
  571.9 2.7 fusion.49
  576.1 63.6 %collective-permute-start.4 = (f32[3,512]{1,0:T(4,128)S(1)}, f32[3,512]{1,0:T(4,128)S(1)}, u32[]{:S(2)}, u32[]{:S(2)}) collective-permute-start(f32[3,512]{1,0:T(4,128)S(1)} %slice.203), channel_id=1, source_target_pairs={{0,1},{1,2},{2,3},{3,4},{4,5},{5,6},{6,7},{7,8},{8,9},{9,10},{10,1... | collective-permute-start | bytes 18440 | tf_op jit(solution)/shard_map/ppermute | solution.py:16
  641.8 62.4 %psum.31 = f32[]{:T(128)} all-reduce(f32[]{:T(128)} %multiply_reduce_fusion), channel_id=1, replica_groups=mesh['runs'=2,'grp'=4,'mem'=4] {'grp','mem'}, use_global_device_ids=true, to_apply=%region_19.20 | all-reduce | flops 1 | bytes 8 | tf_op jit(solution)/shard_map/psum | solution.py:91
  (463 shorter events, 172.1 us)
Async XLA Ops:
  0.6 0.7 slice-start
  0.6 3.4 copy-start.4
  1.4 1.3 copy-start.2
  1.4 8.5 %collective-permute-start = (f32[3,3,512]{2,1,0:T(4,128)S(1)}, f32[3,3,512]{2,1,0:T(4,128)S(1)}, u32[]{:S(2)}, u32[]{:S(2)}) collective-permute-start(f32[3,3,512]{2,1,0:T(4,128)S(1)} %copy.10), channel_id=1, source_target_pairs={{1,0},{2,1},{3,2},{4,3},{5,4},{6,5},{7,6},{8,7},{9,8},{10,9},{11,1... | collective-permute-start | bytes 55304 | tf_op jit(solution)/shard_map/ppermute | solution.py:16
  2.7 7.2 %collective-permute-start.1 = (f32[3,512]{1,0:T(4,128)S(1)}, f32[3,512]{1,0:T(4,128)S(1)}, u32[]{:S(2)}, u32[]{:S(2)}) collective-permute-start(f32[3,512]{1,0:T(4,128)S(1)} %slice.196), channel_id=1, source_target_pairs={{1,0},{2,1},{3,2},{4,3},{5,4},{6,5},{7,6},{8,7},{9,8},{10,9},{11,1... | collective-permute-start | bytes 18440 | tf_op jit(solution)/shard_map/ppermute | solution.py:16
  9.9 0.7 copy-start
  9.9 0.7 copy-start.1
  9.9 0.7 copy-start.5
  212.0 65.0 %collective-permute-start.2 = (f32[3,512]{1,0:T(4,128)S(1)}, f32[3,512]{1,0:T(4,128)S(1)}, u32[]{:S(2)}, u32[]{:S(2)}) collective-permute-start(f32[3,512]{1,0:T(4,128)S(1)} %slice.199), channel_id=1, source_target_pairs={{0,1},{1,2},{2,3},{3,4},{4,5},{5,6},{6,7},{7,8},{8,9},{9,10},{10,1... | collective-permute-start | bytes 18440 | tf_op jit(solution)/shard_map/ppermute | solution.py:16
  275.6 1.5 copy-start.3
  369.1 5.5 collective-permute-start.3
  576.1 65.0 %collective-permute-start.4 = (f32[3,512]{1,0:T(4,128)S(1)}, f32[3,512]{1,0:T(4,128)S(1)}, u32[]{:S(2)}, u32[]{:S(2)}) collective-permute-start(f32[3,512]{1,0:T(4,128)S(1)} %slice.203), channel_id=1, source_target_pairs={{0,1},{1,2},{2,3},{3,4},{4,5},{5,6},{6,7},{7,8},{8,9},{9,10},{10,1... | collective-permute-start | bytes 18440 | tf_op jit(solution)/shard_map/ppermute | solution.py:16
where the time goes:
time: 717 us; the launch traced here: 706 us
  matrix products  168 us (23%)
  blocking collectives  151 us (21%)
  loops' own time  137 us (19%)
  starting transfers between devices  131 us (18%)
  other arithmetic  59.1 us (8%)
  local copies, waits for them, and re-layouts  42.5 us (6%)
  waiting for transfers between devices  12.7 us (2%)
    another operation x16, loops' own time, row_step(): return lax.fori_loop(0, tile_count[block], tile_step, partial_value)  137 us
    ppermute x5, starting transfers between devices, from_behind(): return lax.ppermute(value, axis, pairs)  131 us
    dot_general x38, matrix products, tile_step(): jnp.dot(kernel_tile, window[target], precision=PRECISE)  102 us
    psum x2, blocking collectives, squares(): return lax.psum(jnp.sum(residual * residual), ('grp', 'mem'))  88.1 us
    dot_general x38, matrix products, tile_step(): jnp.dot(own_vector, kernel_tile, precision=PRECISE)  65.7 us
    psum x1, blocking collectives, local(): curvature = lax.psum(jnp.sum(direction * image), ('grp', 'mem'))  62.4 us
    another operation x108, other arithmetic  56.5 us
    dynamic_slice x38, local copies, waits for them, and re-layouts, tile_step(): block_row = tiles[block, slot, 0]  24.9 us
  transfers between devices with their start and end apart: 5, of which 4 were waited for; matrix products, arithmetic and copies ran while one was open for 0% of the time, Pallas kernels for 0%

commit v1 on v0

v1 whole, which is shorter than its diff:
```python
import functools

import jax
import jax.numpy as jnp
from jax import lax
from jax.experimental import pallas as pl
from jax.experimental.pallas import tpu as pltpu
from jax.sharding import PartitionSpec as P

SCALE = 0.2 * 16.0
TINY = 1e-30
LANES = 128
SUBLANES = 8
UNROLL = 16
AXES = ("grp", "mem")
MIB = 1 << 20
X, Y, T, V, COUNT = range(5)

VMEM = pl.BlockSpec(memory_space=pltpu.VMEM)
SMEM = pl.BlockSpec(memory_space=pltpu.SMEM)


def resident(*arrays):
    return [pltpu.with_memory_space_constraint(a, pltpu.VMEM) for a in arrays]


def call(kernel, out_shape, operands, specs, scratch=(), limit=12):
    return pl.pallas_call(
        kernel,
        out_shape=out_shape,
        in_specs=specs,
        out_specs=jax.tree.map(lambda _: VMEM, out_shape),
        scratch_shapes=list(scratch),
        compiler_params=pltpu.CompilerParams(vmem_limit_bytes=limit * MIB),
    )(*operands)


def shape(*dims):
    return jax.ShapeDtypeStruct(dims, jnp.float32)


def vmem(*dims):
    return pltpu.VMEM(dims, jnp.float32)


def entries(xi, yi, ti, xj, yj, tj, mode):
    dx = xi - xj
    dy = yi - yj
    u = jnp.maximum(dx * dx + dy * dy, TINY)
    s = u * lax.rsqrt(u)
    a = jnp.maximum(1.0 - s, 0.0)
    if mode == "same":
        d = jnp.abs(ti - tj)
        b = 1.0 - d
        f = d + 0.25
    elif mode == "any":
        d = jnp.abs(ti - tj)
        b = jnp.maximum(1.0 - d, 0.0)
        f = d + 0.25
    else:
        b = jnp.maximum(ti - tj, 0.0) if mode == "next" else jnp.maximum(tj - ti, 0.0)
        f = 1.25 - b
    p = a * b
    p = p * p
    return (p * p) * ((s + 0.25) * f)


def spread(row):
    return jnp.broadcast_to(row, (SUBLANES, row.shape[-1]))


def tile(make, load, rows_of, width, sum_ref, col_add, chunks_of, unroll=UNROLL):
    chunks = width // LANES

    def band(lo, hi, used, single):
        def step(it, acc):
            acc = list(acc)
            for uu in range(unroll):
                at = pl.ds(pl.multiple_of((it * unroll + uu) * SUBLANES, SUBLANES), SUBLANES)
                row = rows_of(at)
                total = None
                for q, ch in enumerate(used):
                    m = make(row, at, ch)
                    w = m * load(ch)
                    total = w if total is None else total + w
                    if col_add is not None and ch != single:
                        acc[q] = acc[q] + m * row[V]
                sum_ref[at, :] += total
            return tuple(acc)

        zero = jnp.zeros((SUBLANES, LANES), jnp.float32)
        acc = lax.fori_loop(
            lo // (SUBLANES * unroll), hi // (SUBLANES * unroll), step, tuple(zero for _ in used)
        )
        if col_add is not None:
            for q, ch in enumerate(used):
                if ch != single:
                    col_add(ch, acc[q])

    if chunks_of == "upper":
        for ri in range(chunks):
            band(ri * LANES, (ri + 1) * LANES, list(range(ri, chunks)), ri)
    else:
        band(0, width, list(range(chunks)), -1)


def cut(ch):
    return pl.ds(ch * LANES, LANES)


def new_tile(r, side, c, slot, mode, k_ref, cols, accl, accs, diag):
    width = side.shape[-1]
    chunks = width // LANES
    right = [[spread(side[c, q : q + 1, cut(ch)]) for ch in range(chunks)] for q in (X, Y, T, V)]
    if mode == "prev":
        right[T] = [t + 1.0 for t in right[T]]

    def rows_of(at):
        row = [cols[q, r, at, :] for q in (X, Y, T, V)]
        if mode == "next":
            row[T] = row[T] + 1.0
        return row

    def make(row, at, ch):
        m = entries(row[X], row[Y], row[T], right[X][ch], right[Y][ch], right[T][ch], mode)
        k_ref[slot, at, cut(ch)] = m
        return m

    col_add = None
    if accs is not None:

        def col_add(ch, value):
            accs[c, :, cut(ch)] += value

    tile(make, lambda ch: right[V][ch], rows_of, width, accl.at[r], col_add, "upper" if diag else "")


def old_tile(r, side, c, slot, k_ref, vcol, accl, accs, diag):
    width = side.shape[-1]
    chunks = width // LANES
    right = [spread(side[c, 0:1, cut(ch)]) for ch in range(chunks)]

    def rows_of(at):
        return {V: None if vcol is None else vcol[r, at, :]}

    col_add = None
    if accs is not None:

        def col_add(ch, value):
            accs[c, :, cut(ch)] += value

    tile(
        lambda row, at, ch: k_ref[slot, at, cut(ch)],
        lambda ch: right[ch],
        rows_of,
        width,
        accl.at[r],
        col_add,
        "upper" if diag else "",
    )


def inner_tiles(blocks, reach, count, body):
    base = 0
    for k in range(reach + 1):

        def step(r, _, k=k, base=base):
            pl.when(count[r] > k)(lambda: body(r, r + k, base + r, k))
            return 0

        lax.fori_loop(0, blocks - k, step, 0)
        base += blocks - k


def outer_tiles(blocks, reach, count, low_count, body):
    base = 0
    for k in range(1, reach + 1):

        def low(j, _, k=k, base=base):
            at = reach - k + j
            pl.when(low_count(at) > k)(lambda: body(j, 0, at, base + j, k))
            return 0

        def high(j, _, k=k, base=base):
            r = blocks - k + j
            pl.when(count[r] > k)(lambda: body(r, 1, j, base + k + j, k))
            return 0

        lax.fori_loop(0, k, low, 0)
        lax.fori_loop(0, k, high, 0)
        base += 2 * k


def pack_kernel(count, coords, vector, first, last, rows):
    blocks, _, width = rows.shape
    edge = first.shape[0]
    for b in range(blocks):
        rows[b, X : T + 1, :] = coords[b]
        rows[b, V : V + 1, :] = vector[b : b + 1, :]
        rows[b, COUNT:, :] = jnp.full((SUBLANES - COUNT, width), count[b].astype(jnp.float32))
    first[...] = rows[0:edge]
    last[...] = rows[blocks - edge :]


def inner_kernel(reach, count, packed, k_ref, cols, accl, accs, rows):
    blocks, _, width = packed.shape
    start = jnp.floor(packed[0, T : T + 1, 0:1])
    rows[...] = packed[...]
    for b in range(blocks):
        rows[b, T : T + 1, :] = packed[b, T : T + 1, :] - start

    def build(b, _):
        flat = rows[b].T
        for q in (X, Y, T, V):
            cols[q, b] = jnp.broadcast_to(flat[:, q : q + 1], (width, LANES))
        return 0

    lax.fori_loop(0, blocks, build, 0)
    accl[...] = jnp.zeros_like(accl)
    accs[...] = jnp.zeros_like(accs)

    def body(r, c, slot, k):
        mode = ("same", "any")[k] if k < 2 else "next"
        new_tile(r, rows, c, slot, mode, k_ref, cols, accl, accs, k == 0)

    inner_tiles(blocks, reach, count, body)


def outer_kernel(reach, count, low_in, high_in, packed, noise, cols, accl_in, accs, kx, image, first, last, low, high, accl):
    blocks = packed.shape[0]
    start = jnp.floor(packed[0, T : T + 1, 0:1])
    low[...] = low_in[...]
    high[...] = high_in[...]
    for b in range(reach):
        low[b, T : T + 1, :] = low_in[b, T : T + 1, :] - start
        high[b, T : T + 1, :] = high_in[b, T : T + 1, :] - start
    accl[...] = accl_in[...]

    def low_count(at):
        return jnp.max(low[at, COUNT : COUNT + 1, 0:LANES])

    def body(r, which, c, slot, k):
        mode = "any" if k == 1 else ("prev", "next")[which]
        new_tile(r, (low, high)[which], c, slot, mode, kx, cols, accl, None, False)

    outer_tiles(blocks, reach, count, low_count, body)
    summed = jnp.sum(accs[...], axis=1) + jnp.sum(accl[...], axis=-1)
    image[...] = noise[...] * packed[:, V, :] + SCALE * summed
    first[...] = image[0:reach, :]
    last[...] = image[blocks - reach :, :]


def again_kernel(reach, count, image, k_ref, accl, accs, rows, vcol):
    blocks, width = image.shape
    flat = image[...].T
    for b in range(blocks):
        rows[b, 0:1, :] = image[b : b + 1, :]
        vcol[b] = jnp.broadcast_to(flat[:, b : b + 1], (width, LANES))
    accl[...] = jnp.zeros_like(accl)
    accs[...] = jnp.zeros_like(accs)

    def body(r, c, slot, k):
        old_tile(r, rows, c, slot, k_ref, vcol, accl, accs, k == 0)

    inner_tiles(blocks, reach, count, body)


def dots(pairs):
    lane = lax.broadcasted_iota(jnp.int32, (1, LANES), 1)
    out = jnp.zeros((1, LANES), jnp.float32)
    for n, (a, b) in enumerate(pairs):
        total = jnp.sum(jnp.sum(a * b, axis=1, keepdims=True), axis=0, keepdims=True)
        out = jnp.where(lane == n, total, out)
    return out


def close_kernel(reach, count, low_in, high_in, low_packed, vector, noise, image, kx, accl_in, accs, again, sums, low, high, accl):
    blocks = image.shape[0]
    for b in range(reach):
        low[b, 0:1, :] = low_in[b : b + 1, :]
        high[b, 0:1, :] = high_in[b : b + 1, :]
    accl[...] = accl_in[...]

    def low_count(at):
        return jnp.max(low_packed[at, COUNT : COUNT + 1, 0:LANES])

    def body(r, which, c, slot, k):
        old_tile(r, (low, high)[which], c, slot, kx, None, accl, None, False)

    outer_tiles(blocks, reach, count, low_count, body)
    summed = jnp.sum(accs[...], axis=1) + jnp.sum(accl[...], axis=-1)
    q = image[...]
    p = noise[...] * q + SCALE * summed
    again[...] = p
    b = vector[...]
    sums[...] = jnp.broadcast_to(dots([(b, b), (b, q), (q, q), (b, p), (q, p)]), sums.shape)


def finish_kernel(sums, vector, image, again, solution, residual):
    total = jnp.sum(sums[...], axis=0, keepdims=True)
    bb, bq, qq, bp, qp = [total[:, n : n + 1] for n in range(5)]
    alpha = bb / bq
    rq = bq - alpha * qq
    rr = (bb - alpha * bq) - alpha * rq
    beta = rr / bb
    r_ar = rq - alpha * (bp - alpha * qp)
    b_ar = bq - alpha * bp
    curvature = r_ar + beta * (rq + b_ar) + beta * beta * bq
    gamma = rr / curvature
    b, q, p = vector[...], image[...], again[...]
    r = b - alpha * q
    d = r + beta * b
    ad = (q - alpha * p) + beta * q
    solution[...] = alpha * b + gamma * d
    residual[...] = r - gamma * ad


def shift(value, by):
    length = lax.axis_size(AXES)
    return lax.ppermute(value, AXES, [(i, i + by) for i in range(length) if 0 <= i + by < length])


def local(coords, noise, right_side, tiles, tile_count):
    blocks, width = right_side.shape
    reach = tiles.shape[1] - 1
    inner = sum(blocks - k for k in range(reach + 1))
    outer = reach * (reach + 1)

    first, last, packed = call(
        pack_kernel,
        (shape(reach, SUBLANES, width), shape(reach, SUBLANES, width), vmem(blocks, SUBLANES, width)),
        (tile_count, coords, right_side),
        [SMEM, VMEM, VMEM],
    )
    low = shift(last, 1)
    high = shift(first, -1)
    (packed,) = resident(packed)
    k_in, cols, accl, accs = call(
        functools.partial(inner_kernel, reach),
        (
            vmem(inner, width, width),
            vmem(4, blocks, width, LANES),
            vmem(blocks, width, LANES),
            vmem(blocks, SUBLANES, width),
        ),
        (tile_count, packed),
        [SMEM, VMEM],
        [vmem(blocks, SUBLANES, width)],
    )
    cols, accl, accs = resident(cols, accl, accs)
    k_out, image, first, last = call(
        functools.partial(outer_kernel, reach),
        (vmem(outer, width, width), shape(blocks, width), shape(reach, width), shape(reach, width)),
        (tile_count, low, high, packed, noise, cols, accl, accs),
        [SMEM] + [VMEM] * 7,
        [vmem(reach, SUBLANES, width), vmem(reach, SUBLANES, width), vmem(blocks, width, LANES)],
    )
    image_low = shift(last, 1)
    image_high = shift(first, -1)
    (k_in,) = resident(k_in)
    accl, accs = call(
        functools.partial(again_kernel, reach),
        (vmem(blocks, width, LANES), vmem(blocks, SUBLANES, width)),
        (tile_count, image, k_in),
        [SMEM, VMEM, VMEM],
        [vmem(blocks, SUBLANES, width), vmem(blocks, width, LANES)],
    )
    k_out, accl, accs = resident(k_out, accl, accs)
    devices = lax.axis_size(AXES)
    again, sums = call(
        functools.partial(close_kernel, reach),
        (shape(blocks, width), shape(devices, LANES)),
        (tile_count, image_low, image_high, low, right_side, noise, image, k_out, accl, accs),
        [SMEM] + [VMEM] * 9,
        [vmem(reach, SUBLANES, width), vmem(reach, SUBLANES, width), vmem(blocks, width, LANES)],
    )
    sums = lax.all_to_all(sums, AXES, 0, 0, tiled=True)
    return call(
        finish_kernel,
        (shape(blocks, width), shape(blocks, width)),
        (sums, right_side, image, again),
        [VMEM] * 4,
    )


def solution(mesh):
    in_specs = (
        P(("runs", "grp", "mem"), None, None),
        P(("runs", "grp", "mem"), None),
        P(("runs", "grp", "mem"), None),
        P(("runs", "grp", "mem"), None, None),
        P(("runs", "grp", "mem")),
    )
    out_specs = (P(("runs", "grp", "mem"), None), P(("runs", "grp", "mem"), None))
    return jax.shard_map(local, mesh=mesh, in_specs=in_specs, out_specs=out_specs, check_vma=False)
```

time: 717 us -> 85 us (0.12); the launches traced: 706 us -> 84.6 us
  matrix products: 168 us -> 0 us
  blocking collectives: 151 us -> 12.7 us
  loops' own time: 137 us -> 0 us
  starting transfers between devices: 131 us -> 16.1 us
  other arithmetic: 59.1 us -> 0 us
  Pallas kernels: 0 us -> 34.4 us
  local copies, waits for them, and re-layouts: 42.5 us -> 20.7 us
  waiting for transfers between devices: 12.7 us -> 0.01 us
    dot_general x76 -> x0, matrix products: 168 us -> none  [the longest x38 102 us: tile_step(): jnp.dot(kernel_tile, window[target], precision=PRECISE)]
    psum x3 -> x0, blocking collectives: 151 us -> none  [the longest x2 88.1 us: squares(): return lax.psum(jnp.sum(residual * residual), ('grp', 'mem'))]
    another operation x18 -> x0, loops' own time: 137 us -> none  [the longest x16 137 us: row_step(): return lax.fori_loop(0, tile_count[block], tile_step, partial_value)]
    ppermute x5 -> x4, starting transfers between devices: 131 us -> 16.1 us  [shift(): lax.ppermute(value, AXES, [(i, i + by) for i in range(length) if 0 <= i +...]
    another operation x108 -> x0, other arithmetic: 56.5 us -> none
    dynamic_slice x70 -> x0, local copies, waits for them, and re-layouts: 35.7 us -> none  [the longest x38 24.9 us: tile_step(): block_row = tiles[block, slot, 0]]
    pallas_call x0 -> x6, Pallas kernels: none -> 34.4 us  [call(): pl.pallas_call(kernel, out_shape=out_shape, in_specs=specs, out_specs=jax...]
    unnamed x14 -> x15, local copies, waits for them, and re-layouts: 0.73 us -> 20.7 us
  transfers between devices with their start and end apart: 5 -> 4, of which waited for: 4 -> 0; matrix products, arithmetic and copies ran while one was open for 0% -> 0% of each run, Pallas kernels for 0% -> 29%
where the time goes in v1:
time: 85 us; the launch traced here: 84.6 us
  Pallas kernels  34.4 us (40%)
  local copies, waits for them, and re-layouts  20.7 us (24%)
  starting transfers between devices  16.1 us (19%)
  blocking collectives  12.7 us (15%)
    pallas_call x6, Pallas kernels, call(): pl.pallas_call(kernel, out_shape=out_shape, in_specs=specs, out_specs=jax...  34.4 us
    unnamed x15, local copies, waits for them, and re-layouts  20.7 us
    ppermute x4, starting transfers between devices, shift(): lax.ppermute(value, AXES, [(i, i + by) for i in range(length) if 0 <= i +...  16.1 us
    all_to_all x1, blocking collectives, local(): sums = lax.all_to_all(sums, AXES, 0, 0, tiled=True)  12.7 us
  transfers between devices with their start and end apart: 4, of which 0 were waited for; matrix products, arithmetic and copies ran while one was open for 0% of the time, Pallas kernels for 29%

profile of v1, /device:TPU:0, one launch (start us, length us, event | category | flops | bytes accessed | tf_op | source)
XLA Modules:
  0.0 84.6 jit_solution(13548519777511188489)
XLA Ops:
  0.6 0.8 copy.7.coords
  1.5 0.0 copy-start.2
  1.5 0.7 copy-done.2
  2.2 0.0 copy-start.6
  2.2 0.7 copy-done.6
  2.8 0.6 shard_map.59
  3.4 4.9 %collective-permute-start = (f32[3,8,512]{2,1,0:T(8,128)S(1)}, f32[3,8,512]{2,1,0:T(8,128)S(1)}, u32[]{:S(2)}, u32[]{:S(2)}) collective-permute-start(f32[3,8,512]{2,1,0:T(8,128)S(1)} %get-tuple-element.17), channel_id=1, source_target_pairs={{0,1},{1,2},{2,3},{3,4},{4,5},{5,6},{6,7},{7,8},{8,9},{9,10},{10,1... | collective-permute-start | bytes 147464 | tf_op jit(solution)/shard_map/ppermute | solution.py:320
  8.4 1.3 %collective-permute-start.1 = (f32[3,8,512]{2,1,0:T(8,128)S(1)}, f32[3,8,512]{2,1,0:T(8,128)S(1)}, u32[]{:S(2)}, u32[]{:S(2)}) collective-permute-start(f32[3,8,512]{2,1,0:T(8,128)S(1)} %get-tuple-element.18), channel_id=1, source_target_pairs={{1,0},{2,1},{3,2},{4,3},{5,4},{6,5},{7,6},{8,7},{9,8},{10,9},{11,1... | collective-permute-start | bytes 147464 | tf_op jit(solution)/shard_map/ppermute | solution.py:320
  9.7 20.3 %shard_map.60 = (f32[26,512,512]{2,1,0:T(8,128)S(1)}, f32[4,8,512,128]{3,2,1,0:T(8,128)S(1)}, f32[8,512,128]{2,1,0:T(8,128)S(1)}, f32[8,8,512]{2,1,0:T(8,128)S(1)}) custom-call(s32[8]{0:T(128)S(1)} %copy-done.6, f32[8,8,512]{2,1,0:T(8,128)S(1)} %get-tuple-element.19.packed), custom_call_target="tpu_custom_call" | custom-call | tf_op jit(solution)/shard_map/pallas_call | solution.py:28
  30.0 0.0 copy-start
  30.0 9.0 %copy-done = f32[26,512,512]{2,1,0:T(8,128)} copy-done((f32[26,512,512]{2,1,0:T(8,128)}, f32[26,512,512]{2,1,0:T(8,128)S(1)}, u32[]{:S(2)}) %copy-start) | copy-done | bytes 27263000
  39.0 0.0 collective-permute-done.low_in.low_packed
  39.0 0.0 collective-permute-done.1.high_in
  39.0 0.0 copy-start.4
  39.0 0.7 copy-done.4
  39.7 5.3 %shard_map.61 = (f32[12,512,512]{2,1,0:T(8,128)S(1)}, f32[8,512]{1,0:T(8,128)S(1)}, f32[3,512]{1,0:T(4,128)S(1)}, f32[3,512]{1,0:T(4,128)S(1)}) custom-call(s32[8]{0:T(128)S(1)} %copy-done.6, f32[3,8,512]{2,1,0:T(8,128)S(1)} %collective-permute-done.low_in.low_packed, f32[3,8,512]{2,1,0:T(8,128)S(1)} %collective-permute-done.1.high_in, ...), custom_call_target="tpu_custom_call" | custom-call | tf_op jit(solution)/shard_map/pallas_call | solution.py:28
  45.0 8.6 %collective-permute-start.2 = (f32[3,512]{1,0:T(4,128)S(1)}, f32[3,512]{1,0:T(4,128)S(1)}, u32[]{:S(2)}, u32[]{:S(2)}) collective-permute-start(f32[3,512]{1,0:T(4,128)S(1)} %get-tuple-element.23), channel_id=1, source_target_pairs={{0,1},{1,2},{2,3},{3,4},{4,5},{5,6},{6,7},{7,8},{8,9},{9,10},{10,1... | collective-permute-start | bytes 18440 | tf_op jit(solution)/shard_map/ppermute | solution.py:320
  53.6 1.3 %collective-permute-start.3 = (f32[3,512]{1,0:T(4,128)S(1)}, f32[3,512]{1,0:T(4,128)S(1)}, u32[]{:S(2)}, u32[]{:S(2)}) collective-permute-start(f32[3,512]{1,0:T(4,128)S(1)} %get-tuple-element.24), channel_id=1, source_target_pairs={{1,0},{2,1},{3,2},{4,3},{5,4},{6,5},{7,6},{8,7},{9,8},{10,9},{11,1... | collective-permute-start | bytes 18440 | tf_op jit(solution)/shard_map/ppermute | solution.py:320
  54.9 0.0 copy-start.1
  54.9 8.7 %copy-done.1 = f32[26,512,512]{2,1,0:T(8,128)S(1)} copy-done((f32[26,512,512]{2,1,0:T(8,128)S(1)}, f32[26,512,512]{2,1,0:T(8,128)}, u32[]{:S(2)}) %copy-start.1) | copy-done | bytes 27263000
  63.7 0.0 copy-start.3
  63.7 0.0 copy-start.5
  63.7 4.5 %shard_map.62 = (f32[8,512,128]{2,1,0:T(8,128)S(1)}, f32[8,8,512]{2,1,0:T(8,128)S(1)}) custom-call(s32[8]{0:T(128)S(1)} %copy-done.6, f32[8,512]{1,0:T(8,128)S(1)} %get-tuple-element.25.image, f32[26,512,512]{2,1,0:T(8,128)S(1)} %copy-done.1), custom_call_target="tpu_custom_call" | custom-call | tf_op jit(solution)/shard_map/pallas_call | solution.py:28
  68.2 0.0 collective-permute-done.2.low_in
  68.2 0.0 collective-permute-done.3.high_in
  68.2 0.0 copy-done.3
  68.2 0.0 copy-done.5
  68.2 2.7 %shard_map.63 = (f32[8,512]{1,0:T(8,128)S(1)}, f32[16,128]{1,0:T(8,128)S(1)}) custom-call(s32[8]{0:T(128)S(1)} %copy-done.6, f32[3,512]{1,0:T(4,128)S(1)} %collective-permute-done.2.low_in, f32[3,512]{1,0:T(4,128)S(1)} %collective-permute-done.3.high_in, f32[3,8,512]{2,1,0:T(8,128)S(1)} %collective-permute-done.low_in.low_packed, f32[8,512]{1,0:T(8,128)S(1)} %copy-done.3, ...), custom_call_target="tpu_custom_call" | custom-call | tf_op jit(solution)/shard_map/pallas_call | solution.py:28
  70.9 12.7 %all_to_all.11 = f32[16,1,128]{2,1,0:T(1,128)S(1)} all-to-all(f32[16,1,128]{2,1,0:T(1,128)S(1)} %bitcast.5), channel_id=1, replica_groups=mesh['runs'=2,'grp'=4,'mem'=4] {'grp','mem'}, dimensions={0} | all-to-all | bytes 16384 | tf_op jit(solution)/shard_map/all_to_all | solution.py:377
  83.6 1.0 %shard_map.64 = (f32[8,512]{1,0:T(8,128)}, f32[8,512]{1,0:T(8,128)}) custom-call(f32[16,128]{1,0:T(8,128)S(1)} %bitcast.4, f32[8,512]{1,0:T(8,128)S(1)} %copy-done.3, f32[8,512]{1,0:T(8,128)S(1)} %get-tuple-element.25.image, f32[8,512]{1,0:T(8,128)S(1)} %get-tuple-element.31.again), custom_call_target="tpu_custom_call" | custom-call | tf_op jit(solution)/shard_map/pallas_call | solution.py:28
Async XLA Ops:
  1.5 0.7 copy-start.2
  2.2 0.7 copy-start.6
  3.4 35.6 %collective-permute-start = (f32[3,8,512]{2,1,0:T(8,128)S(1)}, f32[3,8,512]{2,1,0:T(8,128)S(1)}, u32[]{:S(2)}, u32[]{:S(2)}) collective-permute-start(f32[3,8,512]{2,1,0:T(8,128)S(1)} %get-tuple-element.17), channel_id=1, source_target_pairs={{0,1},{1,2},{2,3},{3,4},{4,5},{5,6},{6,7},{7,8},{8,9},{9,10},{10,1... | collective-permute-start | bytes 147464 | tf_op jit(solution)/shard_map/ppermute | solution.py:320
  8.4 30.7 %collective-permute-start.1 = (f32[3,8,512]{2,1,0:T(8,128)S(1)}, f32[3,8,512]{2,1,0:T(8,128)S(1)}, u32[]{:S(2)}, u32[]{:S(2)}) collective-permute-start(f32[3,8,512]{2,1,0:T(8,128)S(1)} %get-tuple-element.18), channel_id=1, source_target_pairs={{1,0},{2,1},{3,2},{4,3},{5,4},{6,5},{7,6},{8,7},{9,8},{10,9},{11,1... | collective-permute-start | bytes 147464 | tf_op jit(solution)/shard_map/ppermute | solution.py:320
  30.0 9.0 %copy-start = (f32[26,512,512]{2,1,0:T(8,128)}, f32[26,512,512]{2,1,0:T(8,128)S(1)}, u32[]{:S(2)}) copy-start(f32[26,512,512]{2,1,0:T(8,128)S(1)} %get-tuple-element.27.k_ref) | copy-start | bytes 81788928
  39.0 0.7 copy-start.4
  45.0 23.2 %collective-permute-start.2 = (f32[3,512]{1,0:T(4,128)S(1)}, f32[3,512]{1,0:T(4,128)S(1)}, u32[]{:S(2)}, u32[]{:S(2)}) collective-permute-start(f32[3,512]{1,0:T(4,128)S(1)} %get-tuple-element.23), channel_id=1, source_target_pairs={{0,1},{1,2},{2,3},{3,4},{4,5},{5,6},{6,7},{7,8},{8,9},{9,10},{10,1... | collective-permute-start | bytes 18440 | tf_op jit(solution)/shard_map/ppermute | solution.py:320
  53.6 14.6 %collective-permute-start.3 = (f32[3,512]{1,0:T(4,128)S(1)}, f32[3,512]{1,0:T(4,128)S(1)}, u32[]{:S(2)}, u32[]{:S(2)}) collective-permute-start(f32[3,512]{1,0:T(4,128)S(1)} %get-tuple-element.24), channel_id=1, source_target_pairs={{1,0},{2,1},{3,2},{4,3},{5,4},{6,5},{7,6},{8,7},{9,8},{10,9},{11,1... | collective-permute-start | bytes 18440 | tf_op jit(solution)/shard_map/ppermute | solution.py:320
  54.9 8.8 %copy-start.1 = (f32[26,512,512]{2,1,0:T(8,128)S(1)}, f32[26,512,512]{2,1,0:T(8,128)}, u32[]{:S(2)}) copy-start(f32[26,512,512]{2,1,0:T(8,128)} %copy-done) | copy-start | bytes 81788928
  63.7 4.5 %copy-start.3 = (f32[8,512]{1,0:T(8,128)S(1)}, f32[8,512]{1,0:T(8,128)}, u32[]{:S(2)}) copy-start(f32[8,512]{1,0:T(8,128)} %vector.5) | copy-start | bytes 49156
  63.7 4.5 %copy-start.5 = (f32[8,512]{1,0:T(8,128)S(1)}, f32[8,512]{1,0:T(8,128)}, u32[]{:S(2)}) copy-start(f32[8,512]{1,0:T(8,128)} %noise.3) | copy-start | bytes 49156

commit v2 on v1

v2 whole, which is shorter than its diff:
```python
import functools

import jax
import jax.numpy as jnp
from jax import lax
from jax.experimental import pallas as pl
from jax.experimental.pallas import tpu as pltpu
from jax.sharding import PartitionSpec as P

SCALE = 0.2 * 16.0
TINY = 1e-30
LANES = 128
SUBLANES = 8
BAND = 128
UNROLL = 16
AXES = ("grp", "mem")
MIB = 1 << 20
X, Y, T, V, N, COUNT = range(6)
NEAR = 4.0
PARTS = ((0, 0), (0, 1), (1, 0), (1, 1), (0, 2), (2, 0))
FEATURES = 32
FIRST_T = 2 * len(PARTS) + 6

VMEM = pl.BlockSpec(memory_space=pltpu.VMEM)
SMEM = pl.BlockSpec(memory_space=pltpu.SMEM)
HBM = pl.BlockSpec(memory_space=pltpu.HBM)


def resident(*arrays):
    return [pltpu.with_memory_space_constraint(a, pltpu.VMEM) for a in arrays]


def call(kernel, out_shape, operands, specs, scratch=(), limit=8, aliases=None):
    return pl.pallas_call(
        kernel,
        out_shape=out_shape,
        in_specs=specs,
        out_specs=jax.tree.map(lambda _: VMEM, out_shape),
        scratch_shapes=list(scratch),
        input_output_aliases=aliases or {},
        compiler_params=pltpu.CompilerParams(vmem_limit_bytes=limit * MIB),
    )(*operands)


def shape(*dims):
    return jax.ShapeDtypeStruct(dims, jnp.float32)


def vmem(*dims, dtype=jnp.float32):
    return pltpu.VMEM(dims, dtype)


def entries(u, ti, tj, mode):
    u = jnp.maximum(u, TINY)
    s = u * lax.rsqrt(u)
    a = jnp.maximum(1.0 - s, 0.0)
    if mode == "same":
        d = jnp.abs(ti - tj)
        b = 1.0 - d
        f = d + 0.25
    elif mode == "any":
        d = jnp.abs(ti - tj)
        b = jnp.maximum(1.0 - d, 0.0)
        f = d + 0.25
    else:
        b = jnp.maximum(ti - tj, 0.0)
        f = 1.25 - b
    p = a * b
    p = p * p
    return (p * p) * ((s + 0.25) * f)


def spread(row):
    return jnp.broadcast_to(row, (SUBLANES, row.shape[-1]))


def cut(ch):
    return slice(ch * LANES, (ch + 1) * LANES)


def split(a):
    high = a.astype(jnp.bfloat16).astype(jnp.float32)
    rest = a - high
    middle = rest.astype(jnp.bfloat16).astype(jnp.float32)
    return [high, middle, rest - middle]


def left_features(x, y):
    xs, ys, norm = split(x), split(y), split(x * x + y * y)
    one = jnp.ones_like(x)
    return [xs[i] for i, _ in PARTS] + [ys[i] for i, _ in PARTS] + norm + [one] * 3


def right_features(x, y):
    xs, ys, norm = split(x), split(y), split(x * x + y * y)
    one = jnp.ones_like(x)
    return [-2.0 * xs[j] for _, j in PARTS] + [-2.0 * ys[j] for _, j in PARTS] + [one] * 3 + norm


def put_right(rt, b, features, flat):
    flat[...] = jnp.zeros_like(flat)
    for q, z in enumerate(features):
        flat[q : q + 1, :] = z[b : b + 1, :]
    rt[b, 0:FEATURES, :] = flat[...].astype(jnp.bfloat16)


def columns(lt, firsts):
    dims = (LANES, LANES * len(firsts))
    row = lax.broadcasted_iota(jnp.int32, dims, 0)
    group = lax.broadcasted_iota(jnp.int32, dims, 1) // LANES
    pick = jnp.zeros(dims, jnp.float32)
    for n, first in enumerate(firsts):
        pick = jnp.where((group == n) & (row >= first) & (row < first + 3), 1.0, pick)
    return jnp.dot(lt, pick.astype(jnp.bfloat16), preferred_element_type=jnp.float32)


def near(x, y):
    return jnp.max(jnp.maximum(jnp.abs(x), jnp.abs(y))) <= NEAR


def new_tile(fill, code, following, mode, diag, side, k_ref, tcol, vcol, accl, accs, bufs):
    slot, r, c = code >> 8, (code >> 4) & 15, code & 15
    width = side.shape[-1]
    chunks = width // LANES
    bands = width // BAND
    tj, vj = [[spread(side[c, q : q + 1, cut(ch)]) for ch in range(chunks)] for q in (T, V)]
    zero = jnp.zeros((SUBLANES, LANES), jnp.float32)
    acc = [zero] * chunks
    for band in range(bands):
        first = band * BAND // LANES if diag else 0
        used = range(first, chunks)
        if band + 1 < bands:
            fill(bufs[(band + 1) % 2], r, c, band + 1, (band + 1) * BAND // LANES if diag else 0)
        else:
            fill(bufs[0], (following >> 4) & 15, following & 15, 0, 0)
        buf = bufs[band % 2]
        for g in range(BAND // SUBLANES):
            near_rows = slice(g * SUBLANES, (g + 1) * SUBLANES)
            at = slice(band * BAND + g * SUBLANES, band * BAND + (g + 1) * SUBLANES)
            ti = tcol[r, at, :]
            if mode == "next":
                ti = ti + 1.0
            if accs is not None:
                vi = vcol[r, at, :]
            total = None
            for ch in used:
                m = entries(buf[near_rows, cut(ch)], ti, tj[ch], mode)
                k_ref[slot, at, cut(ch)] = m
                w = m * vj[ch]
                total = w if total is None else total + w
                if accs is not None and not (diag and ch == first):
                    acc[ch] = acc[ch] + m * vi
            accl[r, at, :] += total
    if accs is not None:
        for ch in range(1 if diag else 0, chunks):
            accs[c, :, cut(ch)] += acc[ch]


def old_tile(code, side, k_ref, vcol, accl, accs, diag):
    slot, r, c = code >> 8, (code >> 4) & 15, code & 15
    width = side.shape[-1]
    chunks = width // LANES
    vj = [spread(side[c, 0:1, cut(ch)]) for ch in range(chunks)]
    zero = jnp.zeros((SUBLANES, LANES), jnp.float32)

    def rows_at(at, acc, used, single):
        acc = list(acc)
        if accs is not None:
            vi = vcol[r, at, :]
        total = None
        for q, ch in enumerate(used):
            m = k_ref[slot, at, cut(ch)]
            w = m * vj[ch]
            total = w if total is None else total + w
            if accs is not None and ch != single:
                acc[q] = acc[q] + m * vi
        accl[r, at, :] += total
        return tuple(acc)

    def band(lo, hi, used, single):
        def step(it, acc):
            for g in range(UNROLL):
                start = pl.multiple_of((it * UNROLL + g) * SUBLANES, SUBLANES)
                acc = rows_at(pl.ds(start, SUBLANES), acc, used, single)
            return acc

        deep = SUBLANES * UNROLL
        acc = lax.fori_loop(lo // deep, hi // deep, step, tuple(zero for _ in used))
        if accs is not None:
            for q, ch in enumerate(used):
                if ch != single:
                    accs[c, :, cut(ch)] += acc[q]

    if diag:
        for ri in range(chunks):
            band(ri * LANES, (ri + 1) * LANES, list(range(ri, chunks)), ri)
    else:
        band(0, width, list(range(chunks)), -1)


def list_inner(blocks, reach, count, todo):
    for r in range(blocks):
        todo[r] = (r << 8) | (r << 4) | r
    ends = [blocks]
    at = jnp.int32(blocks)
    base = 0
    for k in range(1, reach + 1):

        def step(r, at, k=k, base=base):
            todo[at] = ((base + r) << 8) | (r << 4) | (r + k)
            return at + (count[r] > k).astype(jnp.int32)

        at = lax.fori_loop(0, blocks - k, step, at)
        base += blocks - k
        if k == 1:
            ends.append(at)
            base = 0
    todo[at] = 0
    return ends + [at]


def list_outer(blocks, reach, count, low, todo):
    packed_count = jnp.zeros((1, LANES), jnp.float32)
    for at in range(reach):
        packed_count += low[at, COUNT : COUNT + 1, 0:LANES] * float(8**at)
    low_count = jnp.max(packed_count).astype(jnp.int32)
    at = jnp.int32(0)
    slot = 0
    for k in range(1, reach + 1):
        for j in range(k):
            c = reach - k + j
            todo[at] = (slot << 8) | (j << 4) | c
            at += (((low_count >> (3 * c)) & 7) > k).astype(jnp.int32)
            slot += 1
            r = blocks - k + j
            todo[at] = (slot << 8) | (r << 4) | (reach + j)
            at += (count[r] > k).astype(jnp.int32)
            slot += 1
    todo[at] = 0
    return at


def pack_kernel(count_in, coords_in, vector_in, noise_in, first, last, packed, count, coords, vector, noise, sems):
    blocks, _, width = packed.shape
    edge = first.shape[0]
    copies = [
        pltpu.make_async_copy(source, target, sems.at[n])
        for n, (source, target) in enumerate(
            [(count_in, count), (coords_in, coords), (vector_in, vector), (noise_in, noise)]
        )
    ]
    for copy in copies:
        copy.start()
    for copy in copies:
        copy.wait()
    for b in range(blocks):
        for q in (X, Y, T):
            packed[b, q : q + 1, :] = coords[q, b : b + 1, :]
        packed[b, V : V + 1, :] = vector[b : b + 1, :]
        packed[b, N : N + 1, :] = noise[b : b + 1, :]
        packed[b, COUNT:, :] = jnp.full((SUBLANES - COUNT, width), count[b].astype(jnp.float32))
    first[...] = packed[0:edge]
    last[...] = packed[blocks - edge :]


def rows_together(source, q):
    return jnp.concatenate([source[b, q : q + 1, :] for b in range(source.shape[0])], axis=0)


def centre(packed):
    head = packed[0, :, 0:LANES]
    mean = jnp.sum(head, axis=1, keepdims=True) * (1.0 / LANES)
    return mean[X : X + 1], mean[Y : Y + 1], jnp.floor(head[T : T + 1, 0:1])


def matmul_fill(lt, rt):
    def fill(buf, r, c, band, first):
        buf[:, first * LANES :] = jnp.dot(
            lt[r, band * BAND : (band + 1) * BAND, :],
            rt[c, :, first * LANES :],
            preferred_element_type=jnp.float32,
        )

    return fill


def difference_fill(packed, raw):
    def fill(buf, r, c, band, first):
        own = packed[r, :, band * BAND : (band + 1) * BAND].T
        dx = own[:, X : X + 1] - raw[c, X : X + 1, :]
        dy = own[:, Y : Y + 1] - raw[c, Y : Y + 1, :]
        buf[...] = dx * dx + dy * dy

    return fill


def inner_kernel(reach, count, packed, k_same, k_next, k_far, tcol, lt, accl, accs, vcol, rows, rt, flat, buf_a, buf_b, todo):
    blocks, _, width = packed.shape
    cx, cy, start = centre(packed)
    x, y = rows_together(packed, X) - cx, rows_together(packed, Y) - cy
    t, v = rows_together(packed, T) - start, rows_together(packed, V)
    left = left_features(x, y) + split(t) + split(v)
    right = right_features(x, y)
    rt[:, FEATURES:, :] = jnp.zeros((blocks, LANES - FEATURES, width), jnp.bfloat16)
    for b in range(blocks):
        rows[b, T : T + 1, :] = t[b : b + 1, :]
        rows[b, V : V + 1, :] = v[b : b + 1, :]
        flat[...] = jnp.zeros_like(flat)
        for q, z in enumerate(left):
            flat[q : q + 1, :] = z[b : b + 1, :]
        lt[b, :, 0:FEATURES] = flat[...].T.astype(jnp.bfloat16)
        lt[b, :, FEATURES:] = jnp.zeros((width, LANES - FEATURES), jnp.bfloat16)
        put_right(rt, b, right, flat)
    for b in range(blocks):
        both = columns(lt[b], (FIRST_T, FIRST_T + 3))
        tcol[b] = both[:, :LANES]
        vcol[b] = both[:, LANES:]
    accl[...] = jnp.zeros_like(accl)
    accs[...] = jnp.zeros_like(accs)
    ends = list_inner(blocks, reach, count, todo)
    bufs = (buf_a, buf_b)

    def run(fill):
        fill(buf_a, 0, 0, 0, 0)
        begin = 0
        for end, mode, k_ref in zip(ends, ("same", "any", "next"), (k_same, k_next, k_far)):

            def body(n, _, mode=mode, k_ref=k_ref):
                new_tile(fill, todo[n], todo[n + 1], mode, mode == "same", rows, k_ref, tcol, vcol, accl, accs, bufs)
                return 0

            lax.fori_loop(begin, end, body, 0)
            begin = end

    fast = near(x, y)
    pl.when(fast)(lambda: run(matmul_fill(lt, rt)))
    pl.when(jnp.logical_not(fast))(lambda: run(difference_fill(packed, packed)))


def outer_kernel(
    reach, count, low, high, packed, tcol, lt, accl_in, accs,
    kx, image, first, last, accl, raw, rows, rt, flat, buf_a, buf_b, todo,
):
    blocks, _, width = packed.shape
    halo = 2 * reach
    cx, cy, start = centre(packed)
    raw[0:reach] = low[...]
    raw[reach:] = high[...]
    x, y = rows_together(raw, X) - cx, rows_together(raw, Y) - cy
    t = rows_together(raw, T) - start
    right = right_features(x, y)
    rt[:, FEATURES:, :] = jnp.zeros((halo, LANES - FEATURES, width), jnp.bfloat16)
    for b in range(halo):
        rows[b, T : T + 1, :] = t[b : b + 1, :]
        rows[b, V : V + 1, :] = raw[b, V : V + 1, :]
        put_right(rt, b, right, flat)
    end = list_outer(blocks, reach, count, low, todo)
    bufs = (buf_a, buf_b)

    def run(fill):
        code = todo[0]
        fill(buf_a, (code >> 4) & 15, code & 15, 0, 0)

        def body(n, _):
            new_tile(fill, todo[n], todo[n + 1], "any", False, rows, kx, tcol, None, accl, None, bufs)
            return 0

        lax.fori_loop(0, end, body, 0)

    own = jnp.concatenate([rows_together(packed, X) - cx, rows_together(packed, Y) - cy], axis=0)
    fast = jnp.logical_and(near(x, y), near(own, own))
    pl.when(fast)(lambda: run(matmul_fill(lt, rt)))
    pl.when(jnp.logical_not(fast))(lambda: run(difference_fill(packed, raw)))
    summed = jnp.sum(accs[...], axis=1) + jnp.sum(accl[...], axis=-1)
    image[...] = rows_together(packed, N) * rows_together(packed, V) + SCALE * summed
    first[...] = image[0:reach, :]
    last[...] = image[blocks - reach :, :]


def again_kernel(reach, count, image, k_same, k_next, k_far, accl, accs, rows, vcol, flat, todo):
    blocks, width = image.shape
    flat[...] = jnp.zeros_like(flat)
    for n, part in enumerate(split(image[...])):
        for b in range(blocks):
            flat[3 * b + n : 3 * b + n + 1, :] = part[b : b + 1, :]
    lt = flat[...].T.astype(jnp.bfloat16)
    for b in range(blocks):
        rows[b, 0:1, :] = image[b : b + 1, :]
    for b in range(0, blocks, 2):
        both = columns(lt, (3 * b, 3 * b + 3))
        vcol[b] = both[:, :LANES]
        vcol[b + 1] = both[:, LANES:]
    accl[...] = jnp.zeros_like(accl)
    accs[...] = jnp.zeros_like(accs)
    ends = list_inner(blocks, reach, count, todo)
    begin = 0
    for end, k_ref in zip(ends, (k_same, k_next, k_far)):

        def body(n, _, k_ref=k_ref):
            old_tile(todo[n], rows, k_ref, vcol, accl, accs, k_ref is k_same)
            return 0

        lax.fori_loop(begin, end, body, 0)
        begin = end


def dots(pairs):
    lane = lax.broadcasted_iota(jnp.int32, (1, LANES), 1)
    out = jnp.zeros((1, LANES), jnp.float32)
    for n, (a, b) in enumerate(pairs):
        total = jnp.sum(jnp.sum(a * b, axis=1, keepdims=True), axis=0, keepdims=True)
        out = jnp.where(lane == n, total, out)
    return out


def close_kernel(reach, count, low_in, high_in, low, packed, image, kx, accl_in, accs, again, sums, accl, rows, todo):
    blocks = image.shape[0]
    for b in range(reach):
        rows[b, 0:1, :] = low_in[b : b + 1, :]
        rows[reach + b, 0:1, :] = high_in[b : b + 1, :]
    end = list_outer(blocks, reach, count, low, todo)

    def body(n, _):
        old_tile(todo[n], rows, kx, None, accl, None, False)
        return 0

    lax.fori_loop(0, end, body, 0)
    summed = jnp.sum(accs[...], axis=1) + jnp.sum(accl[...], axis=-1)
    q = image[...]
    p = rows_together(packed, N) * q + SCALE * summed
    again[...] = p
    b = rows_together(packed, V)
    sums[...] = jnp.broadcast_to(dots([(b, b), (b, q), (q, q), (b, p), (q, p)]), sums.shape)


def finish_kernel(sums, packed, image, again, solution, residual):
    total = jnp.sum(sums[...], axis=0, keepdims=True)
    bb, bq, qq, bp, qp = [total[:, n : n + 1] for n in range(5)]
    alpha = bb / bq
    rq = bq - alpha * qq
    rr = (bb - alpha * bq) - alpha * rq
    beta = rr / bb
    r_ar = rq - alpha * (bp - alpha * qp)
    b_ar = bq - alpha * bp
    curvature = r_ar + beta * (rq + b_ar) + beta * beta * bq
    gamma = rr / curvature
    b, q, p = rows_together(packed, V), image[...], again[...]
    r = b - alpha * q
    d = r + beta * b
    ad = (q - alpha * p) + beta * q
    solution[...] = alpha * b + gamma * d
    residual[...] = r - gamma * ad


def shift(value, by):
    length = lax.axis_size(AXES)
    return lax.ppermute(value, AXES, [(i, i + by) for i in range(length) if 0 <= i + by < length])


def local(coords, noise, right_side, tiles, tile_count):
    blocks, width = right_side.shape
    reach = tiles.shape[1] - 1
    inner = sum(blocks - k for k in range(reach + 1))
    outer = reach * (reach + 1)
    half = jnp.bfloat16
    bands = [vmem(BAND, width), vmem(BAND, width)]
    todo = pltpu.SMEM((inner + 2,), jnp.int32)

    first, last, packed = call(
        pack_kernel,
        (shape(reach, SUBLANES, width), shape(reach, SUBLANES, width), vmem(blocks, SUBLANES, width)),
        (tile_count, jnp.transpose(coords, (1, 0, 2)), right_side, noise),
        [HBM] * 4,
        [
            pltpu.SMEM((blocks,), jnp.int32),
            vmem(3, blocks, width),
            vmem(blocks, width),
            vmem(blocks, width),
            pltpu.SemaphoreType.DMA((4,)),
        ],
    )
    low = shift(last, 1)
    high = shift(first, -1)
    (packed,) = resident(packed)
    *k_in, tcol, lt, accl, accs = call(
        functools.partial(inner_kernel, reach),
        (
            vmem(blocks, width, width),
            vmem(blocks - 1, width, width),
            vmem(inner - 2 * blocks + 1, width, width),
            vmem(blocks, width, LANES),
            vmem(blocks, width, LANES, dtype=half),
            vmem(blocks, width, LANES),
            vmem(blocks, SUBLANES, width),
        ),
        (tile_count, packed),
        [SMEM, VMEM],
        [
            vmem(blocks, width, LANES),
            vmem(blocks, SUBLANES, width),
            vmem(blocks, LANES, width, dtype=half),
            vmem(FEATURES, width),
            *bands,
            todo,
        ],
    )
    *k_in, tcol, lt, accl, accs = resident(*k_in, tcol, lt, accl, accs)
    k_out, image, first, last, accl = call(
        functools.partial(outer_kernel, reach),
        (
            vmem(outer, width, width),
            vmem(blocks, width),
            shape(reach, width),
            shape(reach, width),
            vmem(blocks, width, LANES),
        ),
        (tile_count, low, high, packed, tcol, lt, accl, accs),
        [SMEM] + [VMEM] * 7,
        [
            vmem(2 * reach, SUBLANES, width),
            vmem(2 * reach, SUBLANES, width),
            vmem(2 * reach, LANES, width, dtype=half),
            vmem(FEATURES, width),
            *bands,
            todo,
        ],
        aliases={6: 4},
    )
    image_low = shift(last, 1)
    image_high = shift(first, -1)
    image, *k_in = resident(image, *k_in)
    accl, accs = call(
        functools.partial(again_kernel, reach),
        (vmem(blocks, width, LANES), vmem(blocks, SUBLANES, width)),
        (tile_count, image, *k_in),
        [SMEM] + [VMEM] * 4,
        [vmem(blocks, SUBLANES, width), vmem(blocks, width, LANES), vmem(LANES, width), todo],
    )
    k_out, accl, accs = resident(k_out, accl, accs)
    devices = lax.axis_size(AXES)
    again, sums, _ = call(
        functools.partial(close_kernel, reach),
        (vmem(blocks, width), shape(devices, LANES), vmem(blocks, width, LANES)),
        (tile_count, image_low, image_high, low, packed, image, k_out, accl, accs),
        [SMEM] + [VMEM] * 8,
        [vmem(2 * reach, SUBLANES, width), todo],
        aliases={7: 2},
    )
    sums = lax.all_to_all(sums, AXES, 0, 0, tiled=True)
    (again,) = resident(again)
    return call(
        finish_kernel,
        (shape(blocks, width), shape(blocks, width)),
        (sums, packed, image, again),
        [VMEM] * 4,
    )


def solution(mesh):
    in_specs = (
        P(("runs", "grp", "mem"), None, None),
        P(("runs", "grp", "mem"), None),
        P(("runs", "grp", "mem"), None),
        P(("runs", "grp", "mem"), None, None),
        P(("runs", "grp", "mem")),
    )
    out_specs = (P(("runs", "grp", "mem"), None), P(("runs", "grp", "mem"), None))
    return jax.shard_map(local, mesh=mesh, in_specs=in_specs, out_specs=out_specs, check_vma=False)
```

time: 85 us -> 64.4 us (0.76)
  local copies, waits for them, and re-layouts: 20.7 us -> 2.88 us
  Pallas kernels: 34.4 us -> 25.5 us
  blocking collectives: 12.7 us -> 17.3 us
  waiting for transfers between devices: 0.01 us -> 2.09 us
    unnamed x15 -> x8, local copies, waits for them, and re-layouts: 20.7 us -> 2.88 us
    pallas_call x6, Pallas kernels: 34.4 us -> 25.5 us  [call(): pl.pallas_call(kernel, out_shape=out_shape, in_specs=specs, out_specs=jax...]
    all_to_all x1, blocking collectives: 12.7 us -> 17.3 us  [local(): sums = lax.all_to_all(sums, AXES, 0, 0, tiled=True)]
    ppermute x4, waiting for transfers between devices: 0.01 us -> 2.09 us  [shift(): lax.ppermute(value, AXES, [(i, i + by) for i in range(length) if 0 <= i +...]
  transfers between devices with their start and end apart: 4 -> 4, of which waited for: 0 -> 1; matrix products, arithmetic and copies ran while one was open for 0% -> 0% of each run, Pallas kernels for 29% -> 30%
where the time goes in v2:
time: 64.4 us
  Pallas kernels  25.5 us (40%)
  blocking collectives  17.3 us (27%)
  starting transfers between devices  15.9 us (25%)
  local copies, waits for them, and re-layouts  2.88 us (4%)
  waiting for transfers between devices  2.09 us (3%)
  between operations  0.72 us (1%)
    pallas_call x6, Pallas kernels, call(): pl.pallas_call(kernel, out_shape=out_shape, in_specs=specs, out_specs=jax...  25.5 us
    all_to_all x1, blocking collectives, local(): sums = lax.all_to_all(sums, AXES, 0, 0, tiled=True)  17.3 us
    ppermute x4, starting transfers between devices, shift(): lax.ppermute(value, AXES, [(i, i + by) for i in range(length) if 0 <= i +...  15.9 us
    unnamed x8, local copies, waits for them, and re-layouts  2.88 us
    ppermute x4, waiting for transfers between devices, shift(): lax.ppermute(value, AXES, [(i, i + by) for i in range(length) if 0 <= i +...  2.09 us
  transfers between devices with their start and end apart: 4, of which 1 were waited for; matrix products, arithmetic and copies ran while one was open for 0% of the time, Pallas kernels for 30%

profile of v2, /device:TPU:0, one launch (start us, length us, event | category | flops | bytes accessed | tf_op | source)
XLA Modules:
  0.0 64.4 jit_solution(9791680564291769141)
XLA Ops:
  0.6 0.0 copy-start
  0.6 0.8 %copy-done = f32[8,3,512]{2,0,1:T(8,128)S(1)} copy-done((f32[8,3,512]{2,0,1:T(8,128)S(1)}, f32[8,3,512]{2,0,1:T(8,128)}, u32[]{:S(2)}) %copy-start) | copy-done | bytes 49176
  1.4 0.0 copy-start.1
  1.4 0.7 %copy-done.1 = f32[8,512]{1,0:T(8,128)S(1)} copy-done((f32[8,512]{1,0:T(8,128)S(1)}, f32[8,512]{1,0:T(8,128)}, u32[]{:S(2)}) %copy-start.1) | copy-done | bytes 16408
  2.1 0.0 copy-start.2
  2.1 0.7 %copy-done.2 = f32[8,512]{1,0:T(8,128)S(1)} copy-done((f32[8,512]{1,0:T(8,128)S(1)}, f32[8,512]{1,0:T(8,128)}, u32[]{:S(2)}) %copy-start.2) | copy-done | bytes 16408
  2.9 0.0 copy-start.3
  2.9 0.7 %copy-done.3 = s32[8]{0:T(128)S(1)} copy-done((s32[8]{0:T(128)S(1)}, s32[8]{0:T(128)}, u32[]{:S(2)}) %copy-start.3) | copy-done | bytes 56
  3.5 0.6 shard_map.59
  4.1 4.9 %collective-permute-start = (f32[3,8,512]{2,1,0:T(8,128)S(1)}, f32[3,8,512]{2,1,0:T(8,128)S(1)}, u32[]{:S(2)}, u32[]{:S(2)}) collective-permute-start(f32[3,8,512]{2,1,0:T(8,128)S(1)} %get-tuple-element.20), channel_id=1, source_target_pairs={{0,1},{1,2},{2,3},{3,4},{4,5},{5,6},{6,7},{7,8},{8,9},{9,10},{10,1... | collective-permute-start | bytes 147464 | tf_op jit(solution)/shard_map/ppermute | solution.py:457
  9.1 1.3 %collective-permute-start.1 = (f32[3,8,512]{2,1,0:T(8,128)S(1)}, f32[3,8,512]{2,1,0:T(8,128)S(1)}, u32[]{:S(2)}, u32[]{:S(2)}) collective-permute-start(f32[3,8,512]{2,1,0:T(8,128)S(1)} %get-tuple-element.21), channel_id=1, source_target_pairs={{1,0},{2,1},{3,2},{4,3},{5,4},{6,5},{7,6},{8,7},{9,8},{10,9},{11,1... | collective-permute-start | bytes 147464 | tf_op jit(solution)/shard_map/ppermute | solution.py:457
  10.4 15.1 %shard_map.60 = (f32[8,512,512]{2,1,0:T(8,128)S(1)}, f32[7,512,512]{2,1,0:T(8,128)S(1)}, f32[11,512,512]{2,1,0:T(8,128)S(1)}, f32[8,512,128]{2,1,0:T(8,128)S(1)}...) custom-call(s32[8]{0:T(128)S(1)} %copy-done.3, ...), custom_call_target="tpu_custom_call" | custom-call | tf_op jit(solution)/shard_map/pallas_call | solution.py:34
  25.5 0.0 collective-permute-done.low
  25.5 0.0 collective-permute-done.1.high
  25.5 3.1 %shard_map.61 = (f32[12,512,512]{2,1,0:T(8,128)S(1)}, f32[8,512]{1,0:T(8,128)S(1)}, f32[3,512]{1,0:T(4,128)S(1)}, f32[3,512]{1,0:T(4,128)S(1)}, f32[8,512,128]{2,1,0:T(8,128)S(1)}) custom-call(s32[8]{0:T(128)S(1)} %copy-done.3, f32[3,8,512]{2,1,0:T(8,128)S(1)} %collective-permute-done.low, ...), custom_call_target="tpu_custom_call", output_to_operand_aliasing={{4}: (6, {})} | custom-call | tf_op jit(solution)/shard_map/pallas_call | solution.py:34
  28.6 8.4 %collective-permute-start.2 = (f32[3,512]{1,0:T(4,128)S(1)}, f32[3,512]{1,0:T(4,128)S(1)}, u32[]{:S(2)}, u32[]{:S(2)}) collective-permute-start(f32[3,512]{1,0:T(4,128)S(1)} %get-tuple-element.27), channel_id=1, source_target_pairs={{0,1},{1,2},{2,3},{3,4},{4,5},{5,6},{6,7},{7,8},{8,9},{9,10},{10,1... | collective-permute-start | bytes 18440 | tf_op jit(solution)/shard_map/ppermute | solution.py:457
  37.1 1.3 %collective-permute-start.3 = (f32[3,512]{1,0:T(4,128)S(1)}, f32[3,512]{1,0:T(4,128)S(1)}, u32[]{:S(2)}, u32[]{:S(2)}) collective-permute-start(f32[3,512]{1,0:T(4,128)S(1)} %get-tuple-element.28), channel_id=1, source_target_pairs={{1,0},{2,1},{3,2},{4,3},{5,4},{6,5},{7,6},{8,7},{9,8},{10,9},{11,1... | collective-permute-start | bytes 18440 | tf_op jit(solution)/shard_map/ppermute | solution.py:457
  38.4 4.0 %shard_map.62 = (f32[8,512,128]{2,1,0:T(8,128)S(1)}, f32[8,8,512]{2,1,0:T(8,128)S(1)}) custom-call(s32[8]{0:T(128)S(1)} %copy-done.3, f32[8,512]{1,0:T(8,128)S(1)} %get-tuple-element.29.image, f32[8,512,512]{2,1,0:T(8,128)S(1)} %get-tuple-element.31.k_same, f32[7,512,512]{2,1,0:T(8,128)S(1)} %get-tuple-element.32.k_next, ...), custom_call_target="tpu_custom_call" | custom-call | tf_op jit(solution)/shard_map/pallas_call | solution.py:34
  42.3 0.0 collective-permute-done.2.low_in
  42.3 2.1 %collective-permute-done.3.high_in = f32[3,512]{1,0:T(4,128)S(1)} collective-permute-done((f32[3,512]{1,0:T(4,128)S(1)}, f32[3,512]{1,0:T(4,128)S(1)}, u32[]{:S(2)}, u32[]{:S(2)}) %collective-permute-start.3) | collective-permute-done | bytes 6176 | tf_op jit(solution)/shard_map/ppermute | solution.py:457
  44.4 1.7 %shard_map.63 = (f32[8,512]{1,0:T(8,128)S(1)}, f32[16,128]{1,0:T(8,128)S(1)}, f32[8,512,128]{2,1,0:T(8,128)S(1)}) custom-call(s32[8]{0:T(128)S(1)} %copy-done.3, f32[3,512]{1,0:T(4,128)S(1)} %collective-permute-done.2.low_in, f32[3,512]{1,0:T(4,128)S(1)} %collective-permute-done.3.high_in, ...), custom_call_target="tpu_custom_call", output_to_operand_aliasing={{2}: (7, {})} | custom-call | tf_op jit(solution)/shard_map/pallas_call | solution.py:34
  46.1 17.3 %all_to_all.11 = f32[16,1,128]{2,1,0:T(1,128)S(1)} all-to-all(f32[16,1,128]{2,1,0:T(1,128)S(1)} %bitcast.7), channel_id=1, replica_groups=mesh['runs'=2,'grp'=4,'mem'=4] {'grp','mem'}, dimensions={0} | all-to-all | bytes 16384 | tf_op jit(solution)/shard_map/all_to_all | solution.py:549
  63.4 1.0 %shard_map.64 = (f32[8,512]{1,0:T(8,128)}, f32[8,512]{1,0:T(8,128)}) custom-call(f32[16,128]{1,0:T(8,128)S(1)} %bitcast.6, f32[8,8,512]{2,1,0:T(8,128)S(1)} %get-tuple-element.22.packed, f32[8,512]{1,0:T(8,128)S(1)} %get-tuple-element.29.image, f32[8,512]{1,0:T(8,128)S(1)} %get-tuple-element.37.again), custom_call_target="tpu_custom_call" | custom-call | tf_op jit(solution)/shard_map/pallas_call | solution.py:34
Async XLA Ops:
  0.6 0.8 %copy-start = (f32[8,3,512]{2,0,1:T(8,128)S(1)}, f32[8,3,512]{2,0,1:T(8,128)}, u32[]{:S(2)}) copy-start(f32[8,3,512]{2,0,1:T(8,128)} %param.5) | copy-start | bytes 147460
  1.4 0.7 %copy-start.1 = (f32[8,512]{1,0:T(8,128)S(1)}, f32[8,512]{1,0:T(8,128)}, u32[]{:S(2)}) copy-start(f32[8,512]{1,0:T(8,128)} %vector_in.1) | copy-start | bytes 49156
  2.1 0.7 %copy-start.2 = (f32[8,512]{1,0:T(8,128)S(1)}, f32[8,512]{1,0:T(8,128)}, u32[]{:S(2)}) copy-start(f32[8,512]{1,0:T(8,128)} %noise_in.1) | copy-start | bytes 49156
  2.9 0.7 %copy-start.3 = (s32[8]{0:T(128)S(1)}, s32[8]{0:T(128)}, u32[]{:S(2)}) copy-start(s32[8]{0:T(128)} %count.7) | copy-start | bytes 100
  4.1 21.4 %collective-permute-start = (f32[3,8,512]{2,1,0:T(8,128)S(1)}, f32[3,8,512]{2,1,0:T(8,128)S(1)}, u32[]{:S(2)}, u32[]{:S(2)}) collective-permute-start(f32[3,8,512]{2,1,0:T(8,128)S(1)} %get-tuple-element.20), channel_id=1, source_target_pairs={{0,1},{1,2},{2,3},{3,4},{4,5},{5,6},{6,7},{7,8},{8,9},{9,10},{10,1... | collective-permute-start | bytes 147464 | tf_op jit(solution)/shard_map/ppermute | solution.py:457
  9.1 16.4 %collective-permute-start.1 = (f32[3,8,512]{2,1,0:T(8,128)S(1)}, f32[3,8,512]{2,1,0:T(8,128)S(1)}, u32[]{:S(2)}, u32[]{:S(2)}) collective-permute-start(f32[3,8,512]{2,1,0:T(8,128)S(1)} %get-tuple-element.21), channel_id=1, source_target_pairs={{1,0},{2,1},{3,2},{4,3},{5,4},{6,5},{7,6},{8,7},{9,8},{10,9},{11,1... | collective-permute-start | bytes 147464 | tf_op jit(solution)/shard_map/ppermute | solution.py:457
  28.6 13.7 %collective-permute-start.2 = (f32[3,512]{1,0:T(4,128)S(1)}, f32[3,512]{1,0:T(4,128)S(1)}, u32[]{:S(2)}, u32[]{:S(2)}) collective-permute-start(f32[3,512]{1,0:T(4,128)S(1)} %get-tuple-element.27), channel_id=1, source_target_pairs={{0,1},{1,2},{2,3},{3,4},{4,5},{5,6},{6,7},{7,8},{8,9},{9,10},{10,1... | collective-permute-start | bytes 18440 | tf_op jit(solution)/shard_map/ppermute | solution.py:457
  37.1 7.4 %collective-permute-start.3 = (f32[3,512]{1,0:T(4,128)S(1)}, f32[3,512]{1,0:T(4,128)S(1)}, u32[]{:S(2)}, u32[]{:S(2)}) collective-permute-start(f32[3,512]{1,0:T(4,128)S(1)} %get-tuple-element.28), channel_id=1, source_target_pairs={{1,0},{2,1},{3,2},{4,3},{5,4},{6,5},{7,6},{8,7},{9,8},{10,9},{11,1... | collective-permute-start | bytes 18440 | tf_op jit(solution)/shard_map/ppermute | solution.py:457
